TPU v7x, 32 devices: a whole 2x2x4 slice. The times are simulated.
32 devices in a mesh: row: 2 (over x), col: 4 (over y, core), mem: 4 (over z).
Axes of the slice: x: 2, y: 2, z: 4, core: 2. Of those that a mesh axis runs over, the one named last changes fastest.
Arguments:
- adj_final: float32 [1024, 4096], P(('mem', 'row'), 'col'), parts along dimension 0, may hold values from -6 to 6
- kappa: float32 [1024, 4096], P(('mem', 'row'), 'col'), parts along dimension 0, may hold values from 0.1 to 1
- elev_early: float32 [1024, 4096], P(('mem', 'row'), 'col'), parts along dimension 0, may hold values from -6 to 6
- elev_late: float32 [1024, 4096], P(('mem', 'row'), 'col'), parts along dimension 0, may hold values from -6 to 6
- basis: bfloat16 [8, 4, 4, 1024, 256], P(('mem', 'row'), 'col'), parts along dimension 0, may hold values from -0.1875 to 0.1875
- basis_index: int32 [8, 4, 512], P(('mem', 'row'), 'col'), parts along dimension 0, may hold values from 0 to 3
- intersection_patch: int32 [8, 4, 512], P(('mem', 'row'), 'col'), parts along dimension 0, may hold values from 0 to 127, as said below
- owner_row: int32 [16, 128], P(('mem', 'col')), parts along dimension 0, may hold values from 0 to 127, as said below
Outputs:
- adj_start: float32 [1024, 4096], P(('mem', 'row'), 'col'), parts along dimension 0
- coeff_grad: float32 [16, 128, 256], P(('mem', 'col'), 'row'), parts along dimension 0
There are 4 independent parts, one for each index of `mem`. A program takes and returns all parts, laid end to end along the dimension named above; each array names one. Nothing has to cross between parts.
Inputs may be any that keep to these rules, and one draw needn't show every extreme that they name: Each row of owner_row is a permutation of 0 to 127; the owner of patch p in strip j is owner_row[j, p] // 64. `intersection_patch`: of the 512 entries of one tile (i, j), at most 512 name patches of any one owner r (patches p with owner_row[j, p] // 64 = r), and exactly 512 name patches of some owner.
All inputs are finite; a program needn't handle non-finite values.
Results may differ from a plain program's by a relative error of at most 0.0029.
Values sent between devices are 32-bit elements; how exact they have to be, the bound alone decides.
A program may use at most 64 MiB of HBM per device.

v0:
```python
import jax
import jax.numpy as jnp
from jax import lax
from jax.sharding import PartitionSpec as P

BS = 32


DT = 0.2


def padded_2(block, sides, width):
    for axis, dim in sides:
        count = lax.axis_size(axis)
        forward = [(i, i + 1) for i in range(count - 1)]
        backward = [(target, source) for source, target in forward]
        low = lax.ppermute(
            lax.slice_in_dim(block, block.shape[dim] - width, None, axis=dim), axis, forward
        )
        high = lax.ppermute(lax.slice_in_dim(block, 0, width, axis=dim), axis, backward)
        block = jnp.concatenate([low, block, high], axis=dim)
    return block


def laplace(padded):
    centre = padded[1:-1, 1:-1]
    return (
        padded[2:, 1:-1] + padded[:-2, 1:-1] + padded[1:-1, 2:] + padded[1:-1, :-2] - 4.0 * centre
    )


def step_once(field, coef):
    bordered = padded_2(field, (("row", 0), ("col", 1)), 1)
    return field + coef * laplace(bordered)


def on_device(
    adj_final, kappa, elev_early, elev_late, basis, basis_index, intersection_patch, owner_row
):
    coef_late = DT * kappa / (1.0 + elev_late * elev_late)
    coef_early = DT * kappa / (1.0 + elev_early * elev_early)
    adj_mid = step_once(adj_final, coef_late)
    adj_start = step_once(adj_mid, coef_early)
    grad_field = (DT * (adj_final + adj_mid)).astype(jnp.bfloat16)
    tile_rows, tile_cols = grad_field.shape
    blocks = grad_field.reshape(tile_rows // BS, BS, tile_cols // BS, BS).transpose(0, 2, 1, 3)
    blocks = blocks.reshape(-1, BS * BS)
    nblock = blocks.shape[0]
    table = basis[0, 0]
    nbasis = table.shape[0]
    products = jnp.einsum("bk,qkn->qbn", blocks, table, preferred_element_type=jnp.float32)
    index = basis_index[0, 0].reshape(nblock, -1)
    select = (index[:, :, None] == jnp.arange(nbasis, dtype=jnp.int32)).astype(jnp.float32)
    contrib = jnp.einsum("boq,qbn->bon", select, products, precision=lax.Precision.HIGHEST)
    contrib = contrib.reshape(-1, contrib.shape[-1])
    strip_rows = owner_row[0]
    n_row = lax.axis_size("row")
    owned_count = strip_rows.shape[0] // n_row
    dest_row = jnp.take(strip_rows, intersection_patch[0, 0])
    count = lax.axis_size("row") * owned_count
    inside = (dest_row >= 0) & (dest_row < count)
    segment = jnp.where(inside, dest_row, count)
    owned = lax.psum_scatter(
        jax.ops.segment_sum(contrib, segment, num_segments=count + 1)[:count],
        "row",
        scatter_dimension=0,
        tiled=True,
    )
    return (adj_start, owned[None])


def solution(mesh):
    return jax.shard_map(
        on_device,
        mesh=mesh,
        in_specs=(
            P(("mem", "row"), "col"),
            P(("mem", "row"), "col"),
            P(("mem", "row"), "col"),
            P(("mem", "row"), "col"),
            P(("mem", "row"), "col", None, None, None),
            P(("mem", "row"), "col", None),
            P(("mem", "row"), "col", None),
            P(("mem", "col"), None),
        ),
        out_specs=(P(("mem", "row"), "col"), P(("mem", "col"), "row", None)),
        check_vma=False,
    )
```

profile of v0, /device:TPU:0, one launch (start us, length us, event | category | flops | bytes accessed | tf_op | source)
XLA Modules:
  0.0 73.1 jit_solution(18310511031494554394)
XLA Ops:
  7.2 0.0 copy-start
  7.2 0.0 copy-start.1
  7.2 0.0 copy-start.3
  7.2 0.0 copy-start.4
  7.2 0.0 reduce-scatter.2.cloned.1.call-start
  7.3 0.9 %fusion.22 = (f32[1,1024]{1,0:T(1,128)S(1)}, f32[1,1024]{1,0:T(1,128)S(1)}) fusion(f32[128,1024]{1,0:T(8,128)} %param.8), kind=kLoop, calls=%fused_computation.52 | loop fusion | bytes 16384 | tf_op jit(solution)/shard_map/slice | solution.py:18
  8.2 1.3 %collective-permute-start = (f32[1,1024]{1,0:T(1,128)S(1)}, f32[1,1024]{1,0:T(1,128)S(1)}, u32[]{:S(2)}, u32[]{:S(2)}) collective-permute-start(f32[1,1024]{1,0:T(1,128)S(1)} %get-tuple-element.11), channel_id=1, source_target_pairs={{16,0},{17,1},{18,2},{19,3},{20,4},{21,5},{22,6},{23,7},{24,8},{25... | collective-permute-start | bytes 12296 | tf_op jit(solution)/shard_map/ppermute | solution.py:20
  9.5 4.8 %collective-permute-start.1 = (f32[1,1024]{1,0:T(1,128)S(1)}, f32[1,1024]{1,0:T(1,128)S(1)}, u32[]{:S(2)}, u32[]{:S(2)}) collective-permute-start(f32[1,1024]{1,0:T(1,128)S(1)} %get-tuple-element.10), channel_id=1, source_target_pairs={{0,16},{1,17},{2,18},{3,19},{4,20},{5,21},{6,22},{7,23},{8,24},{9,... | collective-permute-start | bytes 12296 | tf_op jit(solution)/shard_map/ppermute | solution.py:17
  14.3 0.7 compare_select_fusion
  15.0 3.4 %gather_fusion = s32[512]{0:T(512)S(1)} fusion(s32[128]{0:T(128)} %bitcast.21, s32[1024]{0:T(1024)S(1)} %pad_clamp_fusion), kind=kCustom, calls=%fused_computation | custom fusion | bytes 6144 | tf_op jit(solution)/shard_map/jit(_take)/gather | solution.py:59
  18.5 0.0 collective-permute-done
  18.5 0.0 collective-permute-done.1
  18.5 0.0 copy-done.1
  18.5 0.1 pad_maximum_fusion.21
  18.6 1.3 %collective-permute-start.2 = (f32[130,1]{1,0:T(8,128)S(1)}, f32[130,1]{1,0:T(8,128)S(1)}, u32[]{:S(2)}, u32[]{:S(2)}) collective-permute-start(f32[130,1]{1,0:T(8,128)S(1)} %get-tuple-element.6), channel_id=1, source_target_pairs={{4,0},{8,4},{12,8},{5,1},{9,5},{13,9},{6,2},{10,6},{14,10},{7,3},{... | collective-permute-start | bytes 1568 | tf_op jit(solution)/shard_map/ppermute | solution.py:20
  19.9 3.7 %collective-permute-start.3 = (f32[130,1]{1,0:T(8,128)S(1)}, f32[130,1]{1,0:T(8,128)}, u32[]{:S(2)}, u32[]{:S(2)}) collective-permute-start(f32[130,1]{1,0:T(8,128)S(1)} %get-tuple-element.7), channel_id=1, source_target_pairs={{0,4},{4,8},{8,12},{1,5},{5,9},{9,13},{2,6},{6,10},{10,14},{3,7},{... | collective-permute-start | bytes 1568 | tf_op jit(solution)/shard_map/ppermute | solution.py:17
  23.6 0.0 copy-done.3
  23.6 0.5 broadcast.100
  24.1 0.0 copy-done.4
  24.1 0.7 reduce.3
  24.7 0.1 eq.15
  24.9 0.0 collective-permute-done.2
  24.9 0.0 collective-permute-done.3
  24.9 1.7 %multiply_convert_fusion = (bf16[128,1024]{1,0:T(8,128)(2,1)S(1)}, f32[128,1024]{1,0:T(8,128)S(1)}) fusion(f32[128,1024]{1,0:T(8,128)S(1)} %copy-done.1, f32[1,1024]{1,0:T(1,128)S(1)} %collective-permute-done, f32[1,1024]{1,0:T(1,128)S(1)} %collective-permute-done.1, f32[130,1]{1,0:T(8,128)} %collective-permute-done.3, ...), kind=kLoop, calls=%fused_computation.36 | loop fusion | flops 2883584 | bytes 2368528 | tf_op jit(solution)/shard_map/convert_element_type | solution.py:44
  26.6 1.3 %collective-permute-start.4 = (f32[1,1024]{1,0:T(1,128)S(1)}, f32[1,1024]{1,0:T(1,128)S(1)}, u32[]{:S(2)}, u32[]{:S(2)}) collective-permute-start(f32[1,1024]{1,0:T(1,128)S(1)} %get-tuple-element.9), channel_id=1, source_target_pairs={{16,0},{17,1},{18,2},{19,3},{20,4},{21,5},{22,6},{23,7},{24,8},{25... | collective-permute-start | bytes 12296 | tf_op jit(solution)/shard_map/ppermute | solution.py:20
  27.9 4.5 %collective-permute-start.5 = (f32[1,1024]{1,0:T(1,128)S(1)}, f32[1,1024]{1,0:T(1,128)S(1)}, u32[]{:S(2)}, u32[]{:S(2)}) collective-permute-start(f32[1,1024]{1,0:T(1,128)S(1)} %get-tuple-element.8), channel_id=1, source_target_pairs={{0,16},{1,17},{2,18},{3,19},{4,20},{5,21},{6,22},{7,23},{8,24},{9,... | collective-permute-start | bytes 12296 | tf_op jit(solution)/shard_map/ppermute | solution.py:17
  32.5 1.7 %reshape.86 = bf16[4,32,32,32]{3,2,1,0:T(8,128)(2,1)} reshape(bf16[128,1024]{1,0:T(8,128)(2,1)S(1)} %get-tuple-element.2) | data formatting | bytes 524288 | tf_op jit(solution)/shard_map/reshape | solution.py:46
  34.2 2.6 %copy.17 = bf16[4,32,32,32]{3,1,2,0:T(8,128)(2,1)} copy(bf16[4,32,32,32]{3,2,1,0:T(8,128)(2,1)} %reshape.86) | data formatting | bytes 524288 | tf_op jit(solution)/shard_map/reshape | solution.py:46
  36.8 2.3 %reshape.105 = bf16[128,1024,1]{1,0,2:T(8,128)(2,1)S(1)} reshape(bf16[4,32,32,32]{3,2,1,0:T(8,128)(2,1)} %bitcast.22) | data formatting | bytes 524288 | tf_op jit(solution)/shard_map/reshape | solution.py:47
  39.2 0.0 copy-done
  39.2 0.4 fusion
  39.6 0.0 copy-start.2
  39.6 0.0 collective-permute-done.4
  39.6 0.0 collective-permute-done.5
  39.7 0.7 pad_maximum_fusion.18
  40.4 1.3 %collective-permute-start.6 = (f32[130,1]{1,0:T(8,128)}, f32[130,1]{1,0:T(8,128)S(1)}, u32[]{:S(2)}, u32[]{:S(2)}) collective-permute-start(f32[130,1]{1,0:T(8,128)} %get-tuple-element.4), channel_id=1, source_target_pairs={{4,0},{8,4},{12,8},{5,1},{9,5},{13,9},{6,2},{10,6},{14,10},{7,3},{... | collective-permute-start | bytes 1568 | tf_op jit(solution)/shard_map/ppermute | solution.py:20
  41.7 3.7 %collective-permute-start.7 = (f32[130,1]{1,0:T(8,128)}, f32[130,1]{1,0:T(8,128)S(1)}, u32[]{:S(2)}, u32[]{:S(2)}) collective-permute-start(f32[130,1]{1,0:T(8,128)} %get-tuple-element.5), channel_id=1, source_target_pairs={{0,4},{4,8},{8,12},{1,5},{5,9},{9,13},{2,6},{6,10},{10,14},{3,7},{... | collective-permute-start | bytes 1568 | tf_op jit(solution)/shard_map/ppermute | solution.py:17
  45.3 1.7 %fusion.14 = f32[128,4,256]{2,1,0:T(4,128)} fusion(f32[128,4,256]{2,0,1:T(8,128)S(1)} %fusion, s32[128,4]{1,0:T(8,128)S(1)} %eq.15), kind=kOutput, calls=%fused_computation.33 | convolution fusion | flops 6293504 | bytes 1050624 | tf_op jit(solution)/shard_map/boq,qbn->bon/dot_general | solution.py:54
  47.1 2.0 %reshape.101 = f32[512,256]{1,0:T(8,128)} reshape(f32[128,4,256]{2,1,0:T(4,128)} %fusion.14) | data formatting | bytes 1048576 | tf_op jit(solution)/shard_map/reshape | solution.py:55
  49.1 3.8 %scatter_custom_fusion = f32[129,256]{1,0:T(8,128)S(1)} fusion(s32[512]{0:T(512)S(1)} %bitcast.25, f32[512,256]{1,0:T(8,128)} %reshape.101, f32[]{:T(128)} %constant.11.clone.1), kind=kCustom, calls=%fused_computation.45 | custom fusion | flops 131072 | bytes 132608 | tf_op jit(solution)/shard_map/scatter-add | solution.py:64
  52.9 0.7 slice.80
  53.6 0.0 reduce-scatter.2.cloned.1.call-update
  53.6 0.0 collective-permute-done.6
  53.6 0.0 collective-permute-done.7
  53.6 0.0 copy-done.2
  53.6 2.3 %fusion.5 = f32[128,1024]{1,0:T(8,128)} fusion(f32[128,1024]{1,0:T(8,128)S(1)} %get-tuple-element.3, f32[130,1]{1,0:T(8,128)S(1)} %collective-permute-done.7, f32[1,1024]{1,0:T(1,128)S(1)} %collective-permute-done.4, f32[1,1024]{1,0:T(1,128)S(1)} %collective-permute-done.5, f32[130,1]{1,0:T(8,128)S(1)} %collective-permute-done.6, f32[128,1024]{1,0:T(8,128)} %param.10, ...), kind=kLoop, calls=%fused_computation.9 | loop fusion | flops 2490368 | bytes 2106384 | tf_op jit(solution)/shard_map/add | solution.py:34
  56.0 10.3 %reduce-scatter.2.cloned.1.call-done = f32[64,256]{1,0:T(8,128)} async-done(((f32[128,256]{1,0:T(8,128)}), f32[64,256]{1,0:T(8,128)}) %reduce-scatter.2.cloned.1.call-update) | async-done | bytes 65552 | tf_op jit(solution)/shard_map/reduce_scatter | solution.py:63
  (3 shorter events, 0.0 us)
Async XLA Ops:
  7.2 32.0 %copy-start = (bf16[1,1,4,1024,256]{4,3,2,1,0:T(8,128)(2,1)S(1)}, bf16[1,1,4,1024,256]{4,3,2,1,0:T(8,128)(2,1)}, u32[]{:S(2)}) copy-start(bf16[1,1,4,1024,256]{4,3,2,1,0:T(8,128)(2,1)} %param.12) | copy-start | bytes 6291460
  7.2 11.3 %copy-start.1 = (f32[128,1024]{1,0:T(8,128)S(1)}, f32[128,1024]{1,0:T(8,128)}, u32[]{:S(2)}) copy-start(f32[128,1024]{1,0:T(8,128)} %param.8) | copy-start | bytes 1572868
  7.2 16.4 %copy-start.3 = (s32[1,1,512]{2,1,0:T(1,128)S(1)}, s32[1,1,512]{2,1,0:T(1,128)}, u32[]{:S(2)}) copy-start(s32[1,1,512]{2,1,0:T(1,128)} %param.14) | copy-start | bytes 6148
  7.2 16.9 %copy-start.4 = (s32[1,1,512]{2,1,0:T(1,128)S(1)}, s32[1,1,512]{2,1,0:T(1,128)}, u32[]{:S(2)}) copy-start(s32[1,1,512]{2,1,0:T(1,128)} %param.13) | copy-start | bytes 6148
  7.2 59.0 %reduce-scatter.2.cloned.1.call-start = ((), (), s32[]{:S(2)}) async-start(), calls=%async_computation.1 | async-start | bytes 196608 | tf_op jit(solution)/shard_map/reduce_scatter | solution.py:63
  8.2 10.3 %collective-permute-start = (f32[1,1024]{1,0:T(1,128)S(1)}, f32[1,1024]{1,0:T(1,128)S(1)}, u32[]{:S(2)}, u32[]{:S(2)}) collective-permute-start(f32[1,1024]{1,0:T(1,128)S(1)} %get-tuple-element.11), channel_id=1, source_target_pairs={{16,0},{17,1},{18,2},{19,3},{20,4},{21,5},{22,6},{23,7},{24,8},{25... | collective-permute-start | bytes 12296 | tf_op jit(solution)/shard_map/ppermute | solution.py:20
  9.5 9.0 %collective-permute-start.1 = (f32[1,1024]{1,0:T(1,128)S(1)}, f32[1,1024]{1,0:T(1,128)S(1)}, u32[]{:S(2)}, u32[]{:S(2)}) collective-permute-start(f32[1,1024]{1,0:T(1,128)S(1)} %get-tuple-element.10), channel_id=1, source_target_pairs={{0,16},{1,17},{2,18},{3,19},{4,20},{5,21},{6,22},{7,23},{8,24},{9,... | collective-permute-start | bytes 12296 | tf_op jit(solution)/shard_map/ppermute | solution.py:17
  18.6 6.3 %collective-permute-start.2 = (f32[130,1]{1,0:T(8,128)S(1)}, f32[130,1]{1,0:T(8,128)S(1)}, u32[]{:S(2)}, u32[]{:S(2)}) collective-permute-start(f32[130,1]{1,0:T(8,128)S(1)} %get-tuple-element.6), channel_id=1, source_target_pairs={{4,0},{8,4},{12,8},{5,1},{9,5},{13,9},{6,2},{10,6},{14,10},{7,3},{... | collective-permute-start | bytes 1568 | tf_op jit(solution)/shard_map/ppermute | solution.py:20
  19.9 5.0 %collective-permute-start.3 = (f32[130,1]{1,0:T(8,128)S(1)}, f32[130,1]{1,0:T(8,128)}, u32[]{:S(2)}, u32[]{:S(2)}) collective-permute-start(f32[130,1]{1,0:T(8,128)S(1)} %get-tuple-element.7), channel_id=1, source_target_pairs={{0,4},{4,8},{8,12},{1,5},{5,9},{9,13},{2,6},{6,10},{10,14},{3,7},{... | collective-permute-start | bytes 1568 | tf_op jit(solution)/shard_map/ppermute | solution.py:17
  26.6 13.0 %collective-permute-start.4 = (f32[1,1024]{1,0:T(1,128)S(1)}, f32[1,1024]{1,0:T(1,128)S(1)}, u32[]{:S(2)}, u32[]{:S(2)}) collective-permute-start(f32[1,1024]{1,0:T(1,128)S(1)} %get-tuple-element.9), channel_id=1, source_target_pairs={{16,0},{17,1},{18,2},{19,3},{20,4},{21,5},{22,6},{23,7},{24,8},{25... | collective-permute-start | bytes 12296 | tf_op jit(solution)/shard_map/ppermute | solution.py:20
  27.9 11.7 %collective-permute-start.5 = (f32[1,1024]{1,0:T(1,128)S(1)}, f32[1,1024]{1,0:T(1,128)S(1)}, u32[]{:S(2)}, u32[]{:S(2)}) collective-permute-start(f32[1,1024]{1,0:T(1,128)S(1)} %get-tuple-element.8), channel_id=1, source_target_pairs={{0,16},{1,17},{2,18},{3,19},{4,20},{5,21},{6,22},{7,23},{8,24},{9,... | collective-permute-start | bytes 12296 | tf_op jit(solution)/shard_map/ppermute | solution.py:17
  39.6 14.0 %copy-start.2 = (f32[128,1024]{1,0:T(8,128)S(1)}, f32[128,1024]{1,0:T(8,128)}, u32[]{:S(2)}) copy-start(f32[128,1024]{1,0:T(8,128)} %param.9) | copy-start | bytes 1572868
  40.4 13.2 %collective-permute-start.6 = (f32[130,1]{1,0:T(8,128)}, f32[130,1]{1,0:T(8,128)S(1)}, u32[]{:S(2)}, u32[]{:S(2)}) collective-permute-start(f32[130,1]{1,0:T(8,128)} %get-tuple-element.4), channel_id=1, source_target_pairs={{4,0},{8,4},{12,8},{5,1},{9,5},{13,9},{6,2},{10,6},{14,10},{7,3},{... | collective-permute-start | bytes 1568 | tf_op jit(solution)/shard_map/ppermute | solution.py:20
  41.7 11.9 %collective-permute-start.7 = (f32[130,1]{1,0:T(8,128)}, f32[130,1]{1,0:T(8,128)S(1)}, u32[]{:S(2)}, u32[]{:S(2)}) collective-permute-start(f32[130,1]{1,0:T(8,128)} %get-tuple-element.5), channel_id=1, source_target_pairs={{0,4},{4,8},{8,12},{1,5},{5,9},{9,13},{2,6},{6,10},{10,14},{3,7},{... | collective-permute-start | bytes 1568 | tf_op jit(solution)/shard_map/ppermute | solution.py:17
Sparse Core Ops, SparseCore 0:
  53.7 12.4 reduce-scatter.1
where the time goes:
time: 73.6 us; the launch traced here: 73.1 us
  starting transfers between devices  21.9 us (30%)
  local copies, waits for them, and re-layouts  14.4 us (20%)
  between operations  14.3 us (19%)
  waiting for transfers between devices  10.3 us (14%)
  other arithmetic  10 us (14%)
  matrix products  2.19 us (3%)
    ppermute x4, starting transfers between devices, padded_2(): lax.ppermute(lax.slice_in_dim(block, block.shape[dim] - width, None, axis...  16.7 us
    reduce_scatter x1, waiting for transfers between devices, on_device(): lax.psum_scatter(jax.ops.segment_sum(contrib, segment, num_segments=count...  10.3 us
    ppermute x4, starting transfers between devices, padded_2(): lax.ppermute(lax.slice_in_dim(block, 0, width, axis=dim), axis, backward)  5.14 us
    reshape x2, local copies, waits for them, and re-layouts, on_device(): grad_field.reshape(tile_rows // BS, BS, tile_cols // BS, BS)  4.38 us
    scatter-add x1, other arithmetic, on_device(): jax.ops.segment_sum(contrib, segment, num_segments=count + 1)[:count]  3.8 us
    gather x1, local copies, waits for them, and re-layouts, on_device(): dest_row = jnp.take(strip_rows, intersection_patch[0, 0])  3.45 us
    add x1, other arithmetic, step_once(): return field + coef * laplace(bordered)  2.33 us
    reshape x1, local copies, waits for them, and re-layouts, on_device(): blocks = blocks.reshape(-1, BS * BS)  2.31 us
  transfers between devices with their start and end apart: 9, of which 1 were waited for; matrix products, arithmetic and copies ran while one was open for 32% of the time, Pallas kernels for 0%

commit v1 on v0

v1 whole, which is shorter than its diff:
```python
import functools

import jax
import jax.numpy as jnp
from jax import lax
from jax.experimental import pallas as pl
from jax.experimental.pallas import tpu as pltpu
from jax.sharding import PartitionSpec as P

BS = 32
OV = 4
LANES = 128
DT = 0.2
MESH = pl.DeviceIdType.MESH


def kernel(
    n_row,
    n_col,
    adj_hbm,
    kappa_hbm,
    early_hbm,
    late_hbm,
    basis_hbm,
    index_ref,
    patch_ref,
    owner_ref,
    start_ref,
    grad_ref,
    adj,
    kappa,
    early,
    late,
    basis,
    mid,
    field,
    blocks,
    counts,
    row_out,
    row_in,
    col_out,
    col_in,
    part_out,
    part_in,
    load_sem,
    halo_send,
    halo_recv,
    part_send,
    part_recv,
):
    rows, cols = adj.shape
    tiles = cols // LANES
    group = LANES // BS
    high = rows // BS
    nblock = blocks.shape[0]
    nbasis, depth, ncoef = basis.shape
    owned = grad_ref.shape[0]
    i = lax.axis_index("row")
    j = lax.axis_index("col")
    sides = (
        (i > 0, {"row": i - 1}),
        (i < n_row - 1, {"row": i + 1}),
        (j > 0, {"col": j - 1}),
        (j < n_col - 1, {"col": j + 1}),
    )
    partners = [lax.rem(i + step, n_row) for step in range(1, n_row)]

    loads = [
        pltpu.make_async_copy(source, target, load_sem.at[n])
        for n, (source, target) in enumerate(
            ((adj_hbm, adj), (late_hbm, late), (kappa_hbm, kappa), (early_hbm, early), (basis_hbm, basis))
        )
    ]

    barrier = pltpu.get_barrier_semaphore()
    for partner in partners:
        pl.semaphore_signal(barrier, inc=1, device_id={"row": partner}, device_id_type=MESH)
    for exists, target in sides[2:]:

        @pl.when(exists)
        def _(target=target):
            pl.semaphore_signal(barrier, inc=1, device_id=target, device_id_type=MESH)

    for load in loads:
        load.start()

    def halo(step, side):
        out, into = (row_out, row_in) if side < 2 else (col_out, col_in)
        return pltpu.make_async_remote_copy(
            src_ref=out.at[step, side % 2],
            dst_ref=into.at[step, 1 - side % 2],
            send_sem=halo_send.at[step, side],
            recv_sem=halo_recv.at[step, side ^ 1],
            device_id=sides[side][1],
            device_id_type=MESH,
        )

    def halo_arrival(step, side):
        into = row_in if side < 2 else col_in
        out = row_out if side < 2 else col_out
        return pltpu.make_async_remote_copy(
            src_ref=out.at[step, side % 2],
            dst_ref=into.at[step, side % 2],
            send_sem=halo_send.at[step, side],
            recv_sem=halo_recv.at[step, side],
            device_id=sides[side][1],
            device_id_type=MESH,
        )

    def send_edges(step, ref):
        row_out[step, 0] = ref[0:1, :]
        row_out[step, 1] = ref[rows - 1 : rows, :]
        col_out[step, 0] = ref[:, 0:LANES].T[0:1, :]
        col_out[step, 1] = ref[:, cols - LANES : cols].T[LANES - 1 : LANES, :]
        for side in range(4):

            @pl.when(sides[side][0])
            def _(side=side):
                halo(step, side).start()

    def receive_edges(step):
        for side in range(4):
            into = row_in if side < 2 else col_in

            @pl.when(sides[side][0])
            def _(side=side):
                halo_arrival(step, side).wait_recv()

            @pl.when(jnp.logical_not(sides[side][0]))
            def _(side=side, into=into):
                into[step, side % 2] = jnp.zeros(into.shape[2:], jnp.float32)

    lane = lax.broadcasted_iota(jnp.int32, (rows, LANES), 1)
    line = lax.broadcasted_iota(jnp.int32, (rows, LANES), 0)

    def tile(ref, t):
        return ref[:, t * LANES : (t + 1) * LANES]

    def inner_step(ref, coef, t):
        centre = tile(ref, t)
        up = jnp.where(line == 0, 0.0, pltpu.roll(centre, 1, 0))
        down = jnp.where(line == rows - 1, 0.0, pltpu.roll(centre, rows - 1, 0))
        before = pltpu.roll(tile(ref, t - 1), 1, 1) if t else 0.0
        after = pltpu.roll(tile(ref, t + 1), LANES - 1, 1) if t < tiles - 1 else 0.0
        left = jnp.where(lane == 0, before, pltpu.roll(centre, 1, 1))
        right = jnp.where(lane == LANES - 1, after, pltpu.roll(centre, LANES - 1, 1))
        return centre + coef * (up + down + left + right - 4.0 * centre)

    def column(step, side):
        return jnp.broadcast_to(col_in[step, side], (LANES, rows)).T

    loads[0].wait()
    beside = jnp.where(j > 0, 1, 0) + jnp.where(j < n_col - 1, 1, 0)
    pl.semaphore_wait(barrier, n_row - 1 + beside)

    send_edges(0, adj)

    loads[1].wait()
    loads[2].wait()
    for t in range(tiles):
        at = slice(t * LANES, (t + 1) * LANES)
        coef = DT * kappa[:, at] / (1.0 + late[:, at] * late[:, at])
        late[:, at] = coef
        value = inner_step(adj, coef, t)
        mid[:, at] = value
        field[t * rows : (t + 1) * rows, :] = DT * (adj[:, at] + value)
    loads[3].wait()
    for t in range(tiles):
        at = slice(t * LANES, (t + 1) * LANES)
        early[:, at] = DT * kappa[:, at] / (1.0 + early[:, at] * early[:, at])

    patches = owner_ref.shape[1]
    entries = patch_ref.shape[-1]
    patch = patch_ref[...]
    named = lax.broadcasted_iota(jnp.int32, (patches, entries), 0) == patch
    named = named.astype(jnp.float32).astype(jnp.bfloat16)
    owner = jnp.broadcast_to(owner_ref[...], (16, patches))
    digit = lax.broadcasted_iota(jnp.int32, (16, patches), 0)
    digits = jnp.where(digit == 0, owner // owned, owner % owned).astype(jnp.float32).astype(jnp.bfloat16)
    dest = jnp.dot(digits, named, preferred_element_type=jnp.float32)
    dest = (dest[0:1] * float(owned) + dest[1:2]).astype(jnp.int32)
    to_row = lax.broadcasted_iota(jnp.int32, (patches, entries), 0) == dest
    to_row = to_row.astype(jnp.float32).astype(jnp.bfloat16)
    entry = lax.broadcasted_iota(jnp.int32, (1, entries), 1)
    block = entry // OV
    across = cols // BS
    block_row, block_col = block // across, block % across
    place = (block_col % group) * (high * tiles) + block_row * tiles + block_col // group
    place = index_ref[...] * nblock + place
    from_block = lax.broadcasted_iota(jnp.int32, (nbasis * nblock, entries), 0) == place
    from_block = from_block.astype(jnp.float32).astype(jnp.bfloat16)
    counts[...] = lax.dot_general(
        to_row, from_block, (((1,), (1,)), ((), ())), preferred_element_type=jnp.float32
    ).astype(jnp.bfloat16)

    def add_edges(step, coef, first, last, left, right):
        first(coef[0:1, :] * row_in[step, 0])
        last(coef[rows - 1 : rows, :] * row_in[step, 1])
        left(jnp.where(lane == 0, tile(coef, 0) * column(step, 0), 0.0))
        right(jnp.where(lane == LANES - 1, tile(coef, tiles - 1) * column(step, 1), 0.0))

    def first_mid(delta):
        mid[0:1, :] += delta
        for t in range(tiles):
            field[t * rows : t * rows + 1, :] += DT * tile(delta, t)

    def last_mid(delta):
        mid[rows - 1 : rows, :] += delta
        for t in range(tiles):
            field[(t + 1) * rows - 1 : (t + 1) * rows, :] += DT * tile(delta, t)

    def left_mid(delta):
        mid[:, 0:LANES] += delta
        field[0:rows, :] += DT * delta

    def right_mid(delta):
        mid[:, cols - LANES : cols] += delta
        field[(tiles - 1) * rows : tiles * rows, :] += DT * delta

    receive_edges(0)
    add_edges(0, late, first_mid, last_mid, left_mid, right_mid)
    send_edges(1, mid)

    part = lax.broadcasted_iota(jnp.int32, (high * tiles, LANES), 1) // BS
    for s in range(depth // LANES):
        lines = [
            jnp.concatenate(
                [
                    field[pl.ds(R * BS + s * group + t, tiles, stride=rows), :]
                    for R in range(high)
                ],
                axis=0,
            )
            for t in range(group)
        ]
        for k in range(group):
            out = None
            for t in range(group):
                shift = (t - k) % group * BS
                moved = pltpu.roll(lines[t], shift, 1) if shift else lines[t]
                out = moved if out is None else jnp.where(part == t, moved, out)
            height = high * tiles
            blocks[k * height : (k + 1) * height, s * LANES : (s + 1) * LANES] = out.astype(
                jnp.bfloat16
            )

    loads[4].wait()
    products = jnp.concatenate(
        [
            jnp.dot(blocks[...], basis[q], preferred_element_type=jnp.float32)
            for q in range(nbasis)
        ],
        axis=0,
    )
    upper = products.astype(jnp.bfloat16)
    lower = (products - upper.astype(jnp.float32)).astype(jnp.bfloat16)

    def partial(r):
        mine = counts[pl.ds(pl.multiple_of(r * owned, owned), owned), :]
        return jnp.dot(mine, upper, preferred_element_type=jnp.float32) + jnp.dot(
            mine, lower, preferred_element_type=jnp.float32
        )

    def share(n):
        return pltpu.make_async_remote_copy(
            src_ref=part_out.at[n],
            dst_ref=part_in.at[n],
            send_sem=part_send.at[n],
            recv_sem=part_recv.at[n],
            device_id={"row": partners[n]},
            device_id_type=MESH,
        )

    for n in range(n_row - 1):
        part_out[n] = partial(partners[n])
        share(n).start()
    own = partial(i)

    receive_edges(1)
    for t in range(tiles):
        at = slice(t * LANES, (t + 1) * LANES)
        start_ref[:, at] = inner_step(mid, early[:, at], t)

    def first_start(delta):
        start_ref[0:1, :] += delta

    def last_start(delta):
        start_ref[rows - 1 : rows, :] += delta

    def left_start(delta):
        start_ref[:, 0:LANES] += delta

    def right_start(delta):
        start_ref[:, cols - LANES : cols] += delta

    add_edges(1, early, first_start, last_start, left_start, right_start)

    for n in range(n_row - 1):
        share(n).wait_recv()
        own = own + part_in[n]
    grad_ref[...] = own
    for n in range(n_row - 1):
        share(n).wait_send()
    for step in range(2):
        for side in range(4):

            @pl.when(sides[side][0])
            def _(step=step, side=side):
                halo(step, side).wait_send()


def on_device(
    n_row,
    n_col,
    adj_final,
    kappa,
    elev_early,
    elev_late,
    basis,
    basis_index,
    intersection_patch,
    owner_row,
):
    rows, cols = adj_final.shape
    nbasis, depth, ncoef = basis.shape[2:]
    nblock = rows * cols // depth
    patches = owner_row.shape[1]
    owned = patches // n_row
    anywhere = pl.BlockSpec(memory_space=pl.ANY)
    near = pl.BlockSpec(memory_space=pltpu.VMEM)
    whole = pltpu.VMEM((rows, cols), jnp.float32)
    start, grad = pl.pallas_call(
        functools.partial(kernel, n_row, n_col),
        out_shape=(
            jax.ShapeDtypeStruct((rows, cols), jnp.float32),
            jax.ShapeDtypeStruct((owned, ncoef), jnp.float32),
        ),
        in_specs=[anywhere] * 5 + [near] * 3,
        out_specs=(near, near),
        scratch_shapes=[
            whole,
            whole,
            whole,
            whole,
            pltpu.VMEM((nbasis, depth, ncoef), jnp.bfloat16),
            whole,
            pltpu.VMEM((cols // LANES * rows, LANES), jnp.float32),
            pltpu.VMEM((nblock, depth), jnp.bfloat16),
            pltpu.VMEM((patches, nbasis * nblock), jnp.bfloat16),
            pltpu.VMEM((2, 2, 1, cols), jnp.float32),
            pltpu.VMEM((2, 2, 1, cols), jnp.float32),
            pltpu.VMEM((2, 2, 1, rows), jnp.float32),
            pltpu.VMEM((2, 2, 1, rows), jnp.float32),
            pltpu.VMEM((max(n_row - 1, 1), owned, ncoef), jnp.float32),
            pltpu.VMEM((max(n_row - 1, 1), owned, ncoef), jnp.float32),
            pltpu.SemaphoreType.DMA((5,)),
            pltpu.SemaphoreType.DMA((2, 4)),
            pltpu.SemaphoreType.DMA((2, 4)),
            pltpu.SemaphoreType.DMA((max(n_row - 1, 1),)),
            pltpu.SemaphoreType.DMA((max(n_row - 1, 1),)),
        ],
        compiler_params=pltpu.CompilerParams(
            collective_id=0, has_side_effects=True, vmem_limit_bytes=48 * 2**20
        ),
    )(
        adj_final,
        kappa,
        elev_early,
        elev_late,
        basis[0, 0],
        basis_index[0],
        intersection_patch[0],
        owner_row,
    )
    return (start, grad[None])


def solution(mesh):
    n_row, n_col = mesh.shape["row"], mesh.shape["col"]
    return jax.shard_map(
        functools.partial(on_device, n_row, n_col),
        mesh=mesh,
        in_specs=(
            P(("mem", "row"), "col"),
            P(("mem", "row"), "col"),
            P(("mem", "row"), "col"),
            P(("mem", "row"), "col"),
            P(("mem", "row"), "col", None, None, None),
            P(("mem", "row"), "col", None),
            P(("mem", "row"), "col", None),
            P(("mem", "col"), None),
        ),
        out_specs=(P(("mem", "row"), "col"), P(("mem", "col"), "row", None)),
        check_vma=False,
    )
```

time: 73.6 us -> 20.7 us (0.28)
  starting transfers between devices: 21.9 us -> 0 us
  between operations: 14.3 us -> 0.66 us
  Pallas kernels: 0 us -> 10.4 us
  waiting for transfers between devices: 10.3 us -> 0 us
  other arithmetic: 10 us -> 0 us
  local copies, waits for them, and re-layouts: 14.4 us -> 9.19 us
  matrix products: 2.19 us -> 0 us
    ppermute x8 -> x0, starting transfers between devices: 21.8 us -> none  [the longest x4 16.7 us: padded_2(): lax.ppermute(lax.slice_in_dim(block, block.shape[dim] - width, None, axis...]
    pallas_call x0 -> x1, Pallas kernels: none -> 10.4 us  [on_device(): pl.pallas_call(functools.partial(kernel, n_row, n_col), out_shape=(jax.Sh...]
    reduce_scatter x1 -> x0, waiting for transfers between devices: 10.3 us -> none  [on_device(): lax.psum_scatter(jax.ops.segment_sum(contrib, segment, num_segments=count...]
    reshape x4 -> x0, local copies, waits for them, and re-layouts: 8.72 us -> none  [the longest x2 4.38 us: on_device(): grad_field.reshape(tile_rows // BS, BS, tile_cols // BS, BS)]
    unnamed x11 -> x18, local copies, waits for them, and re-layouts: 0.54 us -> 9.19 us
    scatter-add x1 -> x0, other arithmetic: 3.8 us -> none  [on_device(): jax.ops.segment_sum(contrib, segment, num_segments=count + 1)[:count]]
    gather x1 -> x0, local copies, waits for them, and re-layouts: 3.45 us -> none  [on_device(): dest_row = jnp.take(strip_rows, intersection_patch[0, 0])]
    add x1 -> x0, other arithmetic: 2.33 us -> none  [step_once(): return field + coef * laplace(bordered)]
  transfers between devices with their start and end apart: 9 -> 0, of which waited for: 1 -> 0; matrix products, arithmetic and copies ran while one was open for 32% -> 0% of each run, Pallas kernels for 0% -> 0%
where the time goes in v1:
time: 20.7 us; the launch traced here: 20.3 us
  Pallas kernels  10.4 us (50%)
  local copies, waits for them, and re-layouts  9.19 us (44%)
  between operations  0.66 us (3%)
    pallas_call x1, Pallas kernels, on_device(): pl.pallas_call(functools.partial(kernel, n_row, n_col), out_shape=(jax.Sh...  10.4 us
    unnamed x18, local copies, waits for them, and re-layouts  9.19 us

profile of v1, /device:TPU:0, one launch (start us, length us, event | category | flops | bytes accessed | tf_op | source)
XLA Modules:
  0.0 20.3 jit_solution(17373040276547737695)
XLA Ops:
  0.6 0.0 copy-start
  0.6 1.6 %copy-done = bf16[1,1,4,1024,256]{4,3,2,1,0:T(8,128)(2,1)S(1)} copy-done((bf16[1,1,4,1024,256]{4,3,2,1,0:T(8,128)(2,1)S(1)}, bf16[1,1,4,1024,256]{4,3,2,1,0:T(8,128)(2,1)}, u32[]{:S(2)}) %copy-start) | copy-done | bytes 2097176
  2.2 0.0 copy-start.1
  2.2 1.0 %copy-done.1 = f32[128,1024]{1,0:T(8,128)S(1)} copy-done((f32[128,1024]{1,0:T(8,128)S(1)}, f32[128,1024]{1,0:T(8,128)}, u32[]{:S(2)}) %copy-start.1) | copy-done | bytes 524312
  3.3 0.0 copy-start.2
  3.3 1.0 %copy-done.2 = f32[128,1024]{1,0:T(8,128)S(1)} copy-done((f32[128,1024]{1,0:T(8,128)S(1)}, f32[128,1024]{1,0:T(8,128)}, u32[]{:S(2)}) %copy-start.2) | copy-done | bytes 524312
  4.3 0.0 copy-start.3
  4.3 1.0 %copy-done.3 = f32[128,1024]{1,0:T(8,128)S(1)} copy-done((f32[128,1024]{1,0:T(8,128)S(1)}, f32[128,1024]{1,0:T(8,128)}, u32[]{:S(2)}) %copy-start.3) | copy-done | bytes 524312
  5.4 0.0 copy-start.4
  5.4 1.0 %copy-done.4 = f32[128,1024]{1,0:T(8,128)S(1)} copy-done((f32[128,1024]{1,0:T(8,128)S(1)}, f32[128,1024]{1,0:T(8,128)}, u32[]{:S(2)}) %copy-start.4) | copy-done | bytes 524312
  6.4 0.0 copy-start.5
  6.4 0.7 %copy-done.5 = s32[1,1,512]{2,1,0:T(1,128)S(1)} copy-done((s32[1,1,512]{2,1,0:T(1,128)S(1)}, s32[1,1,512]{2,1,0:T(1,128)}, u32[]{:S(2)}) %copy-start.5) | copy-done | bytes 2072
  7.1 0.0 copy-start.6
  7.1 0.7 %copy-done.6 = s32[1,1,512]{2,1,0:T(1,128)S(1)} copy-done((s32[1,1,512]{2,1,0:T(1,128)S(1)}, s32[1,1,512]{2,1,0:T(1,128)}, u32[]{:S(2)}) %copy-start.6) | copy-done | bytes 2072
  7.8 0.0 copy-start.7
  7.8 0.7 %copy-done.7 = s32[1,128]{1,0:T(1,128)S(1)} copy-done((s32[1,128]{1,0:T(1,128)S(1)}, s32[1,128]{1,0:T(1,128)}, u32[]{:S(2)}) %copy-start.7) | copy-done | bytes 536
  8.4 10.4 %shard_map.95 = (f32[128,1024]{1,0:T(8,128)S(1)}, f32[64,256]{1,0:T(8,128)S(1)}) custom-call(f32[128,1024]{1,0:T(8,128)S(1)} %copy-done.1, f32[128,1024]{1,0:T(8,128)S(1)} %copy-done.2, f32[128,1024]{1,0:T(8,128)S(1)} %copy-done.3, f32[128,1024]{1,0:T(8,128)S(1)} %copy-done.4, bf16[4,1024,256]{2,1,0:T(8,128)(2,1)S(1)} %bitcast.4, s32[1,512]{1,0:T(1,128)S(1)} %bitcast.6, ...), custom_call_target="tpu_custom_call" | custom-call | tf_op jit(solution)/shard_map/pallas_call | solution.py:332
  18.9 0.8 %copy.12 = f32[128,1024]{1,0:T(8,128)} copy(f32[128,1024]{1,0:T(8,128)S(1)} %get-tuple-element.8) | data formatting | bytes 1048576
  19.7 0.6 %copy.13 = f32[1,64,256]{2,1,0:T(8,128)} copy(f32[1,64,256]{2,1,0:T(8,128)S(1)} %bitcast.5) | data formatting | bytes 131072
Async XLA Ops:
  0.6 1.6 %copy-start = (bf16[1,1,4,1024,256]{4,3,2,1,0:T(8,128)(2,1)S(1)}, bf16[1,1,4,1024,256]{4,3,2,1,0:T(8,128)(2,1)}, u32[]{:S(2)}) copy-start(bf16[1,1,4,1024,256]{4,3,2,1,0:T(8,128)(2,1)} %param.12) | copy-start | bytes 6291460
  2.2 1.0 %copy-start.1 = (f32[128,1024]{1,0:T(8,128)S(1)}, f32[128,1024]{1,0:T(8,128)}, u32[]{:S(2)}) copy-start(f32[128,1024]{1,0:T(8,128)} %adj_hbm.1) | copy-start | bytes 1572868
  3.3 1.0 %copy-start.2 = (f32[128,1024]{1,0:T(8,128)S(1)}, f32[128,1024]{1,0:T(8,128)}, u32[]{:S(2)}) copy-start(f32[128,1024]{1,0:T(8,128)} %kappa_hbm.1) | copy-start | bytes 1572868
  4.3 1.0 %copy-start.3 = (f32[128,1024]{1,0:T(8,128)S(1)}, f32[128,1024]{1,0:T(8,128)}, u32[]{:S(2)}) copy-start(f32[128,1024]{1,0:T(8,128)} %early_hbm.1) | copy-start | bytes 1572868
  5.4 1.0 %copy-start.4 = (f32[128,1024]{1,0:T(8,128)S(1)}, f32[128,1024]{1,0:T(8,128)}, u32[]{:S(2)}) copy-start(f32[128,1024]{1,0:T(8,128)} %late_hbm.1) | copy-start | bytes 1572868
  6.4 0.7 %copy-start.5 = (s32[1,1,512]{2,1,0:T(1,128)S(1)}, s32[1,1,512]{2,1,0:T(1,128)}, u32[]{:S(2)}) copy-start(s32[1,1,512]{2,1,0:T(1,128)} %param.13) | copy-start | bytes 6148
  7.1 0.7 %copy-start.6 = (s32[1,1,512]{2,1,0:T(1,128)S(1)}, s32[1,1,512]{2,1,0:T(1,128)}, u32[]{:S(2)}) copy-start(s32[1,1,512]{2,1,0:T(1,128)} %param.14) | copy-start | bytes 6148
  7.8 0.7 %copy-start.7 = (s32[1,128]{1,0:T(1,128)S(1)}, s32[1,128]{1,0:T(1,128)}, u32[]{:S(2)}) copy-start(s32[1,128]{1,0:T(1,128)} %owner_ref.1) | copy-start | bytes 1540

commit v2 on v1

--- a/solution.py
+++ b/solution.py
@@ -22,9 +22,9 @@
     early_hbm,
     late_hbm,
     basis_hbm,
-    index_ref,
-    patch_ref,
-    owner_ref,
+    index_hbm,
+    patch_hbm,
+    owner_hbm,
     start_ref,
     grad_ref,
     adj,
@@ -32,6 +32,9 @@
     early,
     late,
     basis,
+    index_ref,
+    patch_ref,
+    owner_ref,
     mid,
     field,
     blocks,
@@ -68,7 +71,16 @@
     loads = [
         pltpu.make_async_copy(source, target, load_sem.at[n])
         for n, (source, target) in enumerate(
-            ((adj_hbm, adj), (late_hbm, late), (kappa_hbm, kappa), (early_hbm, early), (basis_hbm, basis))
+            (
+                (adj_hbm, adj),
+                (late_hbm, late),
+                (kappa_hbm, kappa),
+                (index_hbm, index_ref),
+                (patch_hbm, patch_ref),
+                (owner_hbm, owner_ref),
+                (early_hbm, early),
+                (basis_hbm, basis),
+            )
         )
     ]
 
@@ -164,11 +176,13 @@
         value = inner_step(adj, coef, t)
         mid[:, at] = value
         field[t * rows : (t + 1) * rows, :] = DT * (adj[:, at] + value)
-    loads[3].wait()
+    loads[6].wait()
     for t in range(tiles):
         at = slice(t * LANES, (t + 1) * LANES)
         early[:, at] = DT * kappa[:, at] / (1.0 + early[:, at] * early[:, at])
 
+    for load in loads[3:6]:
+        load.wait()
     patches = owner_ref.shape[1]
     entries = patch_ref.shape[-1]
     patch = patch_ref[...]
@@ -244,7 +258,7 @@
                 jnp.bfloat16
             )
 
-    loads[4].wait()
+    loads[7].wait()
     products = jnp.concatenate(
         [
             jnp.dot(blocks[...], basis[q], preferred_element_type=jnp.float32)
@@ -335,7 +349,7 @@
             jax.ShapeDtypeStruct((rows, cols), jnp.float32),
             jax.ShapeDtypeStruct((owned, ncoef), jnp.float32),
         ),
-        in_specs=[anywhere] * 5 + [near] * 3,
+        in_specs=[anywhere] * 8,
         out_specs=(near, near),
         scratch_shapes=[
             whole,
@@ -343,6 +357,9 @@
             whole,
             whole,
             pltpu.VMEM((nbasis, depth, ncoef), jnp.bfloat16),
+            pltpu.VMEM(basis_index.shape[1:], jnp.int32),
+            pltpu.VMEM(intersection_patch.shape[1:], jnp.int32),
+            pltpu.VMEM(owner_row.shape, jnp.int32),
             whole,
             pltpu.VMEM((cols // LANES * rows, LANES), jnp.float32),
             pltpu.VMEM((nblock, depth), jnp.bfloat16),
@@ -353,14 +370,14 @@
             pltpu.VMEM((2, 2, 1, rows), jnp.float32),
             pltpu.VMEM((max(n_row - 1, 1), owned, ncoef), jnp.float32),
             pltpu.VMEM((max(n_row - 1, 1), owned, ncoef), jnp.float32),
-            pltpu.SemaphoreType.DMA((5,)),
+            pltpu.SemaphoreType.DMA((8,)),
             pltpu.SemaphoreType.DMA((2, 4)),
             pltpu.SemaphoreType.DMA((2, 4)),
             pltpu.SemaphoreType.DMA((max(n_row - 1, 1),)),
             pltpu.SemaphoreType.DMA((max(n_row - 1, 1),)),
         ],
         compiler_params=pltpu.CompilerParams(
-            collective_id=0, has_side_effects=True, vmem_limit_bytes=48 * 2**20
+            collective_id=0, has_side_effects=True, vmem_limit_bytes=63 * 2**20
         ),
     )(
         adj_final,

time: 20.7 us -> 15.8 us (0.76)
  local copies, waits for them, and re-layouts: 9.19 us -> 3.36 us
  Pallas kernels: 10.4 us -> 11.6 us
    unnamed x18 -> x2, local copies, waits for them, and re-layouts: 9.19 us -> 3.36 us
    pallas_call x1, Pallas kernels: 10.4 us -> 11.6 us  [on_device(): pl.pallas_call(functools.partial(kernel, n_row, n_col), out_shape=(jax.Sh...]
where the time goes in v2:
time: 15.8 us; the launch traced here: 15.6 us
  Pallas kernels  11.6 us (73%)
  local copies, waits for them, and re-layouts  3.36 us (21%)
  between operations  0.64 us (4%)
    pallas_call x1, Pallas kernels, on_device(): pl.pallas_call(functools.partial(kernel, n_row, n_col), out_shape=(jax.Sh...  11.6 us
    unnamed x2, local copies, waits for them, and re-layouts  3.36 us

profile of v2, /device:TPU:0, one launch (start us, length us, event | category | flops | bytes accessed | tf_op | source)
XLA Modules:
  0.0 15.6 jit_solution(13924191157557270458)
XLA Ops:
  0.6 11.6 %shard_map.95 = (f32[128,1024]{1,0:T(8,128)}, f32[64,256]{1,0:T(8,128)}) custom-call(f32[128,1024]{1,0:T(8,128)} %adj_hbm.1, f32[128,1024]{1,0:T(8,128)} %kappa_hbm.1, f32[128,1024]{1,0:T(8,128)} %early_hbm.1, f32[128,1024]{1,0:T(8,128)} %late_hbm.1, bf16[4,1024,256]{2,1,0:T(8,128)(2,1)} %bitcast.4, s32[1,512]{1,0:T(1,128)} %bitcast.6, s32[1,512]{1,0:T(1,128)} %bitcast.7, ...), custom_call_target="tpu_custom_call" | custom-call | tf_op jit(solution)/shard_map/pallas_call | solution.py:346
  12.2 1.9 %copy.12 = f32[128,1024]{1,0:T(8,128)} copy(f32[128,1024]{1,0:T(8,128)} %get-tuple-element.8) | data formatting | bytes 1048576
  14.1 1.5 %copy.13 = f32[1,64,256]{2,1,0:T(8,128)} copy(f32[1,64,256]{2,1,0:T(8,128)} %bitcast.5) | data formatting | bytes 131072

commit v3 on v2

--- a/solution.py
+++ b/solution.py
@@ -25,6 +25,8 @@
     index_hbm,
     patch_hbm,
     owner_hbm,
+    start_hbm,
+    grad_hbm,
     start_ref,
     grad_ref,
     adj,
@@ -93,7 +95,7 @@
         def _(target=target):
             pl.semaphore_signal(barrier, inc=1, device_id=target, device_id_type=MESH)
 
-    for load in loads:
+    for load in loads[:6]:
         load.start()
 
     def halo(step, side):
@@ -162,6 +164,8 @@
         return jnp.broadcast_to(col_in[step, side], (LANES, rows)).T
 
     loads[0].wait()
+    for load in loads[6:]:
+        load.start()
     beside = jnp.where(j > 0, 1, 0) + jnp.where(j < n_col - 1, 1, 0)
     pl.semaphore_wait(barrier, n_row - 1 + beside)
 
@@ -308,11 +312,17 @@
         start_ref[:, cols - LANES : cols] += delta
 
     add_edges(1, early, first_start, last_start, left_start, right_start)
+    stores = [
+        pltpu.make_async_copy(start_ref, start_hbm, load_sem.at[8]),
+        pltpu.make_async_copy(grad_ref, grad_hbm, load_sem.at[9]),
+    ]
+    stores[0].start()
 
     for n in range(n_row - 1):
         share(n).wait_recv()
         own = own + part_in[n]
     grad_ref[...] = own
+    stores[1].start()
     for n in range(n_row - 1):
         share(n).wait_send()
     for step in range(2):
@@ -321,6 +331,25 @@
             @pl.when(sides[side][0])
             def _(step=step, side=side):
                 halo(step, side).wait_send()
+
+    for store in stores:
+        store.wait()
+
+
+def place_results(start_from, grad_from, start_to, grad_to, sem):
+    quarter = start_from.shape[0] // 4
+    copies = [
+        pltpu.make_async_copy(
+            start_from.at[pl.ds(n * quarter, quarter)],
+            start_to.at[pl.ds(n * quarter, quarter)],
+            sem.at[n],
+        )
+        for n in range(4)
+    ] + [pltpu.make_async_copy(grad_from, grad_to, sem.at[4])]
+    for copy in copies:
+        copy.start()
+    for copy in copies:
+        copy.wait()
 
 
 def on_device(
@@ -340,8 +369,7 @@
     nblock = rows * cols // depth
     patches = owner_row.shape[1]
     owned = patches // n_row
-    anywhere = pl.BlockSpec(memory_space=pl.ANY)
-    near = pl.BlockSpec(memory_space=pltpu.VMEM)
+    far = pl.BlockSpec(memory_space=pl.ANY)
     whole = pltpu.VMEM((rows, cols), jnp.float32)
     start, grad = pl.pallas_call(
         functools.partial(kernel, n_row, n_col),
@@ -349,9 +377,11 @@
             jax.ShapeDtypeStruct((rows, cols), jnp.float32),
             jax.ShapeDtypeStruct((owned, ncoef), jnp.float32),
         ),
-        in_specs=[anywhere] * 8,
-        out_specs=(near, near),
+        in_specs=[far] * 8,
+        out_specs=(far, far),
         scratch_shapes=[
+            whole,
+            pltpu.VMEM((owned, ncoef), jnp.float32),
             whole,
             whole,
             whole,
@@ -370,7 +400,7 @@
             pltpu.VMEM((2, 2, 1, rows), jnp.float32),
             pltpu.VMEM((max(n_row - 1, 1), owned, ncoef), jnp.float32),
             pltpu.VMEM((max(n_row - 1, 1), owned, ncoef), jnp.float32),
-            pltpu.SemaphoreType.DMA((8,)),
+            pltpu.SemaphoreType.DMA((10,)),
             pltpu.SemaphoreType.DMA((2, 4)),
             pltpu.SemaphoreType.DMA((2, 4)),
             pltpu.SemaphoreType.DMA((max(n_row - 1, 1),)),
@@ -389,6 +419,17 @@
         intersection_patch[0],
         owner_row,
     )
+    start, grad = pl.pallas_call(
+        place_results,
+        out_shape=(
+            jax.ShapeDtypeStruct(start.shape, jnp.float32),
+            jax.ShapeDtypeStruct(grad.shape, jnp.float32),
+        ),
+        in_specs=[far, far],
+        out_specs=(far, far),
+        scratch_shapes=[pltpu.SemaphoreType.DMA((5,))],
+        compiler_params=pltpu.CompilerParams(vmem_limit_bytes=63 * 2**20),
+    )(start, grad)
     return (start, grad[None])
 
 

time: 15.8 us -> 31.2 us (1.97)
  Pallas kernels: 11.6 us -> 30.4 us
  local copies, waits for them, and re-layouts: 3.36 us -> 0 us
    pallas_call x0 -> x1, Pallas kernels: none -> 19 us  [on_device(): pl.pallas_call(place_results, out_shape=(jax.ShapeDtypeStruct(start.shape...]
    unnamed x2 -> x0, local copies, waits for them, and re-layouts: 3.36 us -> none
where the time goes in v3:
time: 31.2 us; the launch traced here: 31 us
  Pallas kernels  30.4 us (97%)
  between operations  0.64 us (2%)
    pallas_call x1, Pallas kernels, on_device(): pl.pallas_call(place_results, out_shape=(jax.ShapeDtypeStruct(start.shape...  19 us
    pallas_call x1, Pallas kernels, on_device(): pl.pallas_call(functools.partial(kernel, n_row, n_col), out_shape=(jax.Sh...  11.4 us

profile of v3, /device:TPU:0, one launch (start us, length us, event | category | flops | bytes accessed | tf_op | source)
XLA Modules:
  0.0 31.0 jit_solution(18227007847869037089)
XLA Ops:
  0.6 11.4 %shard_map.95 = (f32[128,1024]{1,0:T(8,128)}, f32[64,256]{1,0:T(8,128)}) custom-call(f32[128,1024]{1,0:T(8,128)} %adj_hbm.1, f32[128,1024]{1,0:T(8,128)} %kappa_hbm.1, f32[128,1024]{1,0:T(8,128)} %early_hbm.1, f32[128,1024]{1,0:T(8,128)} %late_hbm.1, bf16[4,1024,256]{2,1,0:T(8,128)(2,1)} %bitcast.4, s32[1,512]{1,0:T(1,128)} %bitcast.5, s32[1,512]{1,0:T(1,128)} %bitcast.6, ...), custom_call_target="tpu_custom_call" | custom-call | tf_op jit(solution)/shard_map/pallas_call | solution.py:374
  12.0 19.0 %shard_map.96 = (f32[128,1024]{1,0:T(8,128)}, f32[64,256]{1,0:T(8,128)}) custom-call(f32[128,1024]{1,0:T(8,128)} %get-tuple-element.6.start_from, f32[64,256]{1,0:T(8,128)} %get-tuple-element.7.grad_from), custom_call_target="tpu_custom_call" | custom-call | tf_op jit(solution)/shard_map/pallas_call | solution.py:422

commit v4 on v3

--- a/solution.py
+++ b/solution.py
@@ -336,20 +336,27 @@
         store.wait()
 
 
-def place_results(start_from, grad_from, start_to, grad_to, sem):
-    quarter = start_from.shape[0] // 4
-    copies = [
-        pltpu.make_async_copy(
-            start_from.at[pl.ds(n * quarter, quarter)],
-            start_to.at[pl.ds(n * quarter, quarter)],
-            sem.at[n],
-        )
-        for n in range(4)
-    ] + [pltpu.make_async_copy(grad_from, grad_to, sem.at[4])]
-    for copy in copies:
-        copy.start()
-    for copy in copies:
-        copy.wait()
+def place_results(start_from, grad_from, start_to, grad_to, start, grad, load_sem, store_sem):
+    half = start.shape[0] // 2
+    pieces = [
+        (start_from.at[pl.ds(n * half, half)], start.at[pl.ds(n * half, half)], start_to.at[pl.ds(n * half, half)])
+        for n in range(2)
+    ] + [(grad_from, grad, grad_to)]
+    loads = [
+        pltpu.make_async_copy(source, held, load_sem.at[n])
+        for n, (source, held, _) in enumerate(pieces)
+    ]
+    stores = [
+        pltpu.make_async_copy(held, target, store_sem.at[n])
+        for n, (_, held, target) in enumerate(pieces)
+    ]
+    for load in loads:
+        load.start()
+    for load, store in zip(loads, stores):
+        load.wait()
+        store.start()
+    for store in stores:
+        store.wait()
 
 
 def on_device(
@@ -427,7 +434,12 @@
         ),
         in_specs=[far, far],
         out_specs=(far, far),
-        scratch_shapes=[pltpu.SemaphoreType.DMA((5,))],
+        scratch_shapes=[
+            whole,
+            pltpu.VMEM((owned, ncoef), jnp.float32),
+            pltpu.SemaphoreType.DMA((3,)),
+            pltpu.SemaphoreType.DMA((3,)),
+        ],
         compiler_params=pltpu.CompilerParams(vmem_limit_bytes=63 * 2**20),
     )(start, grad)
     return (start, grad[None])

time: 31.2 us -> 14 us (0.45)
  Pallas kernels: 30.4 us -> 13.2 us
    pallas_call x1, Pallas kernels: 19 us -> 1.8 us  [on_device(): pl.pallas_call(place_results, out_shape=(jax.ShapeDtypeStruct(start.shape...]
where the time goes in v4:
time: 14 us; the launch traced here: 13.8 us
  Pallas kernels  13.2 us (94%)
  between operations  0.64 us (5%)
    pallas_call x1, Pallas kernels, on_device(): pl.pallas_call(functools.partial(kernel, n_row, n_col), out_shape=(jax.Sh...  11.4 us
    pallas_call x1, Pallas kernels, on_device(): pl.pallas_call(place_results, out_shape=(jax.ShapeDtypeStruct(start.shape...  1.8 us

profile of v4, /device:TPU:0, one launch (start us, length us, event | category | flops | bytes accessed | tf_op | source)
XLA Modules:
  0.0 13.8 jit_solution(11553286092179363423)
XLA Ops:
  0.6 11.4 %shard_map.95 = (f32[128,1024]{1,0:T(8,128)}, f32[64,256]{1,0:T(8,128)}) custom-call(f32[128,1024]{1,0:T(8,128)} %adj_hbm.1, f32[128,1024]{1,0:T(8,128)} %kappa_hbm.1, f32[128,1024]{1,0:T(8,128)} %early_hbm.1, f32[128,1024]{1,0:T(8,128)} %late_hbm.1, bf16[4,1024,256]{2,1,0:T(8,128)(2,1)} %bitcast.4, s32[1,512]{1,0:T(1,128)} %bitcast.5, s32[1,512]{1,0:T(1,128)} %bitcast.6, ...), custom_call_target="tpu_custom_call" | custom-call | tf_op jit(solution)/shard_map/pallas_call | solution.py:381
  12.0 1.8 %shard_map.96 = (f32[128,1024]{1,0:T(8,128)}, f32[64,256]{1,0:T(8,128)}) custom-call(f32[128,1024]{1,0:T(8,128)} %get-tuple-element.6.start_from, f32[64,256]{1,0:T(8,128)} %get-tuple-element.7.grad_from), custom_call_target="tpu_custom_call" | custom-call | tf_op jit(solution)/shard_map/pallas_call | solution.py:429

commit v5 on v4

--- a/solution.py
+++ b/solution.py
@@ -294,7 +294,6 @@
         share(n).start()
     own = partial(i)
 
-    receive_edges(1)
     for t in range(tiles):
         at = slice(t * LANES, (t + 1) * LANES)
         start_ref[:, at] = inner_step(mid, early[:, at], t)
@@ -311,6 +310,7 @@
     def right_start(delta):
         start_ref[:, cols - LANES : cols] += delta
 
+    receive_edges(1)
     add_edges(1, early, first_start, last_start, left_start, right_start)
     stores = [
         pltpu.make_async_copy(start_ref, start_hbm, load_sem.at[8]),

time: 14 us -> 14 us (level)
  no operation moved by 1% of the time
where the time goes in v5:
time: 14 us; the launch traced here: 13.8 us
  Pallas kernels  13.2 us (94%)
  between operations  0.64 us (5%)
    pallas_call x1, Pallas kernels, on_device(): pl.pallas_call(functools.partial(kernel, n_row, n_col), out_shape=(jax.Sh...  11.4 us
    pallas_call x1, Pallas kernels, on_device(): pl.pallas_call(place_results, out_shape=(jax.ShapeDtypeStruct(start.shape...  1.8 us

profile of v5, /device:TPU:0, one launch (start us, length us, event | category | flops | bytes accessed | tf_op | source)
XLA Modules:
  0.0 13.8 jit_solution(10079464620481144525)
XLA Ops:
  0.6 11.4 %shard_map.95 = (f32[128,1024]{1,0:T(8,128)}, f32[64,256]{1,0:T(8,128)}) custom-call(f32[128,1024]{1,0:T(8,128)} %adj_hbm.1, f32[128,1024]{1,0:T(8,128)} %kappa_hbm.1, f32[128,1024]{1,0:T(8,128)} %early_hbm.1, f32[128,1024]{1,0:T(8,128)} %late_hbm.1, bf16[4,1024,256]{2,1,0:T(8,128)(2,1)} %bitcast.4, s32[1,512]{1,0:T(1,128)} %bitcast.5, s32[1,512]{1,0:T(1,128)} %bitcast.6, ...), custom_call_target="tpu_custom_call" | custom-call | tf_op jit(solution)/shard_map/pallas_call | solution.py:381
  12.0 1.8 %shard_map.96 = (f32[128,1024]{1,0:T(8,128)}, f32[64,256]{1,0:T(8,128)}) custom-call(f32[128,1024]{1,0:T(8,128)} %get-tuple-element.6.start_from, f32[64,256]{1,0:T(8,128)} %get-tuple-element.7.grad_from), custom_call_target="tpu_custom_call" | custom-call | tf_op jit(solution)/shard_map/pallas_call | solution.py:429

commit v6 on v4

--- a/solution.py
+++ b/solution.py
@@ -95,7 +95,16 @@
         def _(target=target):
             pl.semaphore_signal(barrier, inc=1, device_id=target, device_id_type=MESH)
 
-    for load in loads[:6]:
+    quarter = rows // 4
+    first = [
+        pltpu.make_async_copy(
+            adj_hbm.at[pl.ds(n * quarter, quarter)],
+            adj.at[pl.ds(n * quarter, quarter)],
+            load_sem.at[10 + n],
+        )
+        for n in range(4)
+    ]
+    for load in first + loads[1:6]:
         load.start()
 
     def halo(step, side):
@@ -163,7 +172,8 @@
     def column(step, side):
         return jnp.broadcast_to(col_in[step, side], (LANES, rows)).T
 
-    loads[0].wait()
+    for load in first:
+        load.wait()
     for load in loads[6:]:
         load.start()
     beside = jnp.where(j > 0, 1, 0) + jnp.where(j < n_col - 1, 1, 0)
@@ -337,10 +347,10 @@
 
 
 def place_results(start_from, grad_from, start_to, grad_to, start, grad, load_sem, store_sem):
-    half = start.shape[0] // 2
+    piece = start.shape[0] // 4
     pieces = [
-        (start_from.at[pl.ds(n * half, half)], start.at[pl.ds(n * half, half)], start_to.at[pl.ds(n * half, half)])
-        for n in range(2)
+        (start_from.at[pl.ds(n * piece, piece)], start.at[pl.ds(n * piece, piece)], start_to.at[pl.ds(n * piece, piece)])
+        for n in range(4)
     ] + [(grad_from, grad, grad_to)]
     loads = [
         pltpu.make_async_copy(source, held, load_sem.at[n])
@@ -407,7 +417,7 @@
             pltpu.VMEM((2, 2, 1, rows), jnp.float32),
             pltpu.VMEM((max(n_row - 1, 1), owned, ncoef), jnp.float32),
             pltpu.VMEM((max(n_row - 1, 1), owned, ncoef), jnp.float32),
-            pltpu.SemaphoreType.DMA((10,)),
+            pltpu.SemaphoreType.DMA((14,)),
             pltpu.SemaphoreType.DMA((2, 4)),
             pltpu.SemaphoreType.DMA((2, 4)),
             pltpu.SemaphoreType.DMA((max(n_row - 1, 1),)),
@@ -437,8 +447,8 @@
         scratch_shapes=[
             whole,
             pltpu.VMEM((owned, ncoef), jnp.float32),
-            pltpu.SemaphoreType.DMA((3,)),
-            pltpu.SemaphoreType.DMA((3,)),
+            pltpu.SemaphoreType.DMA((5,)),
+            pltpu.SemaphoreType.DMA((5,)),
         ],
         compiler_params=pltpu.CompilerParams(vmem_limit_bytes=63 * 2**20),
     )(start, grad)

time: 14 us -> 14.1 us (level)
  no operation moved by 1% of the time
where the time goes in v6:
time: 14.1 us; the launch traced here: 13.9 us
  Pallas kernels  13.3 us (94%)
  between operations  0.64 us (5%)
    pallas_call x1, Pallas kernels, on_device(): pl.pallas_call(functools.partial(kernel, n_row, n_col), out_shape=(jax.Sh...  11.5 us
    pallas_call x1, Pallas kernels, on_device(): pl.pallas_call(place_results, out_shape=(jax.ShapeDtypeStruct(start.shape...  1.85 us

profile of v6, /device:TPU:0, one launch (start us, length us, event | category | flops | bytes accessed | tf_op | source)
XLA Modules:
  0.0 13.9 jit_solution(1838165566753425462)
XLA Ops:
  0.6 11.5 %shard_map.95 = (f32[128,1024]{1,0:T(8,128)}, f32[64,256]{1,0:T(8,128)}) custom-call(f32[128,1024]{1,0:T(8,128)} %adj_hbm.1, f32[128,1024]{1,0:T(8,128)} %kappa_hbm.1, f32[128,1024]{1,0:T(8,128)} %early_hbm.1, f32[128,1024]{1,0:T(8,128)} %late_hbm.1, bf16[4,1024,256]{2,1,0:T(8,128)(2,1)} %bitcast.4, s32[1,512]{1,0:T(1,128)} %bitcast.5, s32[1,512]{1,0:T(1,128)} %bitcast.6, ...), custom_call_target="tpu_custom_call" | custom-call | tf_op jit(solution)/shard_map/pallas_call | solution.py:391
  12.1 1.9 %shard_map.96 = (f32[128,1024]{1,0:T(8,128)}, f32[64,256]{1,0:T(8,128)}) custom-call(f32[128,1024]{1,0:T(8,128)} %get-tuple-element.6.start_from, f32[64,256]{1,0:T(8,128)} %get-tuple-element.7.grad_from), custom_call_target="tpu_custom_call" | custom-call | tf_op jit(solution)/shard_map/pallas_call | solution.py:439
